TPU v7x, 32 devices: a whole 2x2x4 slice. The times are simulated.
32 devices in a mesh: dp: 8 (over y, x, core), seq: 4 (over z).
Axes of the slice: x: 2, y: 2, z: 4, core: 2. Of those that a mesh axis runs over, the one named last changes fastest.
Arguments:
- queries: bfloat16 [8, 512, 4096], P('dp', 'seq'), may hold values from -30 to 30
- keys: bfloat16 [8, 512, 1024], P('dp', 'seq'), may hold values from -6 to 6
- values: bfloat16 [8, 512, 1024], P('dp', 'seq'), may hold values from -6 to 6
- head_weight: bfloat16 [4096, 256], P('dp'), may hold values from -0.5 to 0.5
- value_weight: bfloat16 [4096], P('dp'), may hold values from -0.5 to 0.5
- action_ids: int32 [8, 512], P('dp', 'seq'), may hold values from 0 to 255
- rewards: int32 [8, 512], P('dp', 'seq'), may hold values from -128 to 127
- episode_ids: int32 [8, 4], P('dp'), may hold values from 0 to 2, never falling along the last dimension, each value on 1 to 2 neighbouring positions
Outputs:
- grad_queries: bfloat16 [8, 512, 4096], P('dp', 'seq')
- grad_keys: bfloat16 [8, 512, 1024], P('dp', 'seq')
- grad_values: bfloat16 [8, 512, 1024], P('dp', 'seq')
- grad_head: float32 [4096, 256], P('dp')
- grad_value: float32 [4096], P('dp')
Inputs may be any that keep to these rules, and one draw needn't show every extreme that they name: `episode_ids`: episode numbers never fall along a row; each episode covers 1 to 2 whole blocks, one exactly 2.
All inputs are finite; a program needn't handle non-finite values.
Results may differ from a plain program's by a relative error of at most 0.01.
Values may be sent and summed in bfloat16 or wider, within the bound.
A program may use at most 128 MiB of HBM per device.

v0:
```python
import jax
import jax.numpy as jnp
from jax import lax
from jax.sharding import PartitionSpec as P

HEADS = 32
KV_HEADS = 8
HD = 128
ACTS = 256
BLOCK = 128


GAMMA = 0.99
TAU = 0.7
REWARD_UNIT = 64.0
NEG_FILL = -1e30


def passed_along(x, axis, by):
    count = lax.axis_size(axis)
    pairs = [(i, i + by) for i in range(count) if 0 <= i + by < count]
    return lax.ppermute(x, axis, pairs)


def loss_grads(q_taken, v_now, v_next, reward_row):
    target = reward_row.astype(jnp.float32) / REWARD_UNIT + GAMMA * v_next
    err = q_taken - target
    gap = q_taken - v_now
    weight = jnp.where(gap < 0, 1.0 - TAU, TAU)
    grad_q = (2.0 * err).astype(jnp.bfloat16)
    grad_v = (-2.0 * weight * gap).astype(jnp.bfloat16)
    return (grad_q, grad_v)


def per_device(queries, keys, values, head_weight, value_weight, action_ids, rewards, episode_ids):
    tok_local = queries.shape[1]
    group = HEADS // KV_HEADS
    scale = HD ** (-0.5)
    me = lax.axis_index("seq")
    both = jnp.concatenate([keys[0], values[0]], axis=1)
    before = passed_along(both, "seq", 1)
    weight_full, value_full = (
        lax.all_gather(head_weight, "dp", axis=0, tiled=True),
        lax.all_gather(value_weight, "dp", axis=0, tiled=True),
    )
    episodes = episode_ids[0]
    mine = lax.dynamic_index_in_dim(episodes, me, keepdims=False)
    padded = jnp.concatenate([jnp.full((1,), -1, jnp.int32), episodes, jnp.full((1,), -1, jnp.int32)])
    linked_before = lax.dynamic_index_in_dim(padded, me, keepdims=False) == mine
    linked_after = lax.dynamic_index_in_dim(padded, me + 2, keepdims=False) == mine
    pair = jnp.concatenate([before, both], axis=0)
    width = KV_HEADS * HD
    k_heads = pair[:, :width].reshape(2 * tok_local, KV_HEADS, HD)
    v_heads = pair[:, width:].reshape(2 * tok_local, KV_HEADS, HD)
    q_heads = queries[0].reshape(tok_local, KV_HEADS, group, HD)
    at = jnp.arange(tok_local)
    allowed = jnp.concatenate(
        [jnp.broadcast_to(linked_before, (tok_local, tok_local)), at[None, :] <= at[:, None]], axis=1
    )
    scores = (
        jnp.einsum("tmgd,smd->mgts", q_heads, k_heads, preferred_element_type=jnp.float32) * scale
    )
    scores = jnp.where(allowed, scores, NEG_FILL)
    top = jnp.max(scores, axis=-1, keepdims=True)
    expo = jnp.exp(scores - top)
    probs = expo / jnp.sum(expo, axis=-1, keepdims=True)
    probs_low = probs.astype(jnp.bfloat16)
    mixed = jnp.einsum("mgts,smd->tmgd", probs_low, v_heads, preferred_element_type=jnp.float32)
    attended = mixed.astype(jnp.bfloat16).reshape(tok_local, HEADS * HD)
    shared = lax.all_to_all(attended, "dp", split_axis=1, concat_axis=0, tiled=True)
    q_all = jnp.dot(attended, weight_full, preferred_element_type=jnp.float32)
    onehot = (action_ids[0][:, None] == jnp.arange(ACTS)[None, :]).astype(jnp.float32)
    q_taken = jnp.sum(q_all * onehot, axis=1)
    v_now = jnp.dot(attended, value_full, preferred_element_type=jnp.float32)
    v_after = passed_along(v_now[:1], "seq", -1)
    v_after = jnp.where(linked_after, v_after, 0.0)
    v_next = jnp.concatenate([v_now[1:], v_after])
    grad_q, grad_v = loss_grads(q_taken, v_now, v_next, rewards[0])
    select = (onehot * grad_q.astype(jnp.float32)[:, None]).astype(jnp.bfloat16)
    grad_att = jnp.dot(select, weight_full.T, preferred_element_type=jnp.float32)
    grad_att = (
        grad_att + grad_v.astype(jnp.float32)[:, None] * value_full.astype(jnp.float32)[None, :]
    ).astype(jnp.bfloat16)
    steer = jnp.concatenate([select, grad_v[:, None]], axis=1)
    steer_all = lax.all_gather(steer, "dp", axis=0, tiled=True)
    part = jnp.dot(shared.T, steer_all, preferred_element_type=jnp.float32)
    part = lax.psum(part, "seq")
    grad_head, grad_value = part[:, :ACTS], part[:, ACTS]
    d_heads = grad_att.reshape(tok_local, KV_HEADS, group, HD)
    d_probs = jnp.einsum("tmgd,smd->mgts", d_heads, v_heads, preferred_element_type=jnp.float32)
    delta = jnp.sum(probs * d_probs, axis=-1, keepdims=True)
    d_scores = (probs * (d_probs - delta) * scale).astype(jnp.bfloat16)
    query_grad = jnp.einsum("mgts,smd->tmgd", d_scores, k_heads, preferred_element_type=jnp.float32)
    key_sum = jnp.einsum("mgts,tmgd->smd", d_scores, q_heads, preferred_element_type=jnp.float32)
    value_sum = jnp.einsum("mgts,tmgd->smd", probs_low, d_heads, preferred_element_type=jnp.float32)
    sums = jnp.concatenate(
        [key_sum.reshape(2 * tok_local, width), value_sum.reshape(2 * tok_local, width)], axis=1
    )
    later = passed_along(sums[:tok_local].astype(jnp.bfloat16), "seq", -1)
    sums = (sums[tok_local:] + later.astype(jnp.float32)).astype(jnp.bfloat16)
    query_low = query_grad.astype(jnp.bfloat16).reshape(tok_local, HEADS * HD)
    return (query_low[None], sums[None, :, :width], sums[None, :, width:], grad_head, grad_value)


def solution(mesh):
    return jax.shard_map(
        per_device,
        mesh=mesh,
        in_specs=(
            P("dp", "seq", None),
            P("dp", "seq", None),
            P("dp", "seq", None),
            P("dp", None),
            P("dp"),
            P("dp", "seq"),
            P("dp", "seq"),
            P("dp", None),
        ),
        out_specs=(
            P("dp", "seq", None),
            P("dp", "seq", None),
            P("dp", "seq", None),
            P("dp", None),
            P("dp"),
        ),
        check_vma=False,
    )
```

profile of v0, /device:TPU:0, one launch (start us, length us, event | category | flops | bytes accessed | tf_op | source)
XLA Modules:
  0.0 137.7 jit_solution(2967684816787529632)
XLA Ops:
  10.2 5.0 %collective-permute-start = (bf16[128,2048]{0,1:T(8,128)(2,1)S(1)}, bf16[128,2048]{0,1:T(8,128)(2,1)S(1)}, u32[]{:S(2)}, u32[]{:S(2)}) collective-permute-start(bf16[128,2048]{0,1:T(8,128)(2,1)S(1)} %pad_maximum_fusion.1), channel_id=1, source_target_pairs={{0,1},{1,2},{2,3},{4,5},{5,6},{6,7},{8,9},{9,10},{10,11},{12,13},{... | collective-permute-start | bytes 1572872 | tf_op jit(solution)/shard_map/ppermute | solution.py:22
  15.2 1.2 constant_dynamic-slice_fusion
  21.0 8.9 %all-gather = bf16[8,1,512]{2,1,0:T(2,128)(2,1)S(1)} all-gather(bf16[1,1,512]{2,1,0:T(2,128)(2,1)S(1)} %reshape.78), channel_id=1, replica_groups=mesh['dp'=8,'seq'=4] {'dp'}, dimensions={0}, use_global_device_ids=true | all-gather | bytes 9216 | tf_op jit(solution)/shard_map/all_gather | solution.py:44
  30.0 1.6 %copy.79 = bf16[1,128,4096]{1,2,0:T(8,128)(2,1)S(1)} copy(bf16[1,128,4096]{2,1,0:T(8,128)(2,1)} %param.8) | data formatting | bytes 2097152 | tf_op jit(solution)/shard_map/reshape;squeeze | solution.py:55
  31.9 3.4 %fusion.40 = (f32[8,4,128]{2,1,0:T(4,128)S(1)}, f32[8,4,128,256]{2,3,1,0:T(8,128)}) fusion(pred[128,256]{0,1:T(8,128)(4,1)S(1)} %concatenate.28, bf16[256,8,128,1]{0,2,3,1:T(8,128)(2,1)S(1)} %bitcast.134, bf16[128,8,4,128]{0,3,2,1:T(8,128)(2,1)S(1)} %bitcast.129), kind=kOutput, calls=%fused_computation.63 | convolution fusion | flops 272630016 | bytes 5816320 | tf_op jit(solution)/shard_map/sub | solution.py:65
  35.3 2.7 %convolution_convert_fusion = bf16[8,128,4,128]{3,1,2,0:T(8,128)(2,1)S(1)} fusion(bf16[256,8,128,1]{0,2,3,1:T(8,128)(2,1)S(1)} %bitcast.127, f32[8,4,128,256]{2,3,1,0:T(8,128)} %get-tuple-element.30, f32[8,4,128]{2,1,0:T(4,128)S(1)} %get-tuple-element.29), kind=kOutput, calls=%fused_computation.21 | convolution fusion | flops 271056896 | bytes 5783552 | tf_op jit(solution)/shard_map/mgts,smd->tmgd/dot_general | solution.py:68
  38.4 1.3 collective-permute-start.1
  39.7 1.4 copy.61
  41.1 3.6 %all-to-all-start = ((bf16[128,8,512]{2,0,1:T(8,128)(2,1)}), bf16[128,8,512]{2,0,1:T(8,128)(2,1)S(1)}, u32[]{:S(2)}, u32[]{:S(2)}) async-start(bf16[128,8,512]{2,0,1:T(8,128)(2,1)} %copy.61), calls=%async_computation | async-start | bytes 2097152 | tf_op jit(solution)/shard_map/all_to_all | solution.py:70
  45.4 2.2 %fusion.14 = f32[128]{0:T(128)S(1)} fusion(bf16[128,4096]{0,1:T(8,128)(2,1)S(1)} %bitcast.119, bf16[4096,256]{1,0:T(8,128)(2,1)} %all-gather.3.cloned.1.call-done, s32[128]{0:T(128)S(1)} %bitcast.139), kind=kOutput, calls=%fused_computation.24 | convolution fusion | flops 268533632 | bytes 3146752 | tf_op jit(solution)/shard_map/dot_general | solution.py:71
  47.7 2.4 %fusion.2 = bf16[128,4096]{1,0:T(8,128)(2,1)S(1)} fusion(bf16[4096,256]{1,0:T(8,128)(2,1)} %all-gather.3.cloned.1.call-done, f32[4096]{0:T(1024)S(1)} %convert_element_type.72, f32[128]{0:T(128)S(1)} %get-tuple-element.20, bf16[128]{0:T(256)(128)(2,1)S(1)} %get-tuple-element.26, s32[128]{0:T(128)S(1)} %bitcast.140), kind=kOutput, calls=%fused_computation.3 | convolution fusion | flops 270073856 | bytes 3163392 | tf_op jit(solution)/shard_map/dot_general | solution.py:80
  50.8 4.0 %fusion.19 = f32[8,128,256,1]{2,1,3,0:T(8,128)} fusion(bf16[128,8,4,128]{0,3,2,1:T(8,128)(2,1)S(1)} %bitcast.121, f32[8,4,128,256]{2,3,1,0:T(8,128)} %get-tuple-element.30, f32[8,4,128]{2,1,0:T(4,128)S(1)} %get-tuple-element.29), kind=kOutput, calls=%fused_computation.32 | convolution fusion | flops 270532608 | bytes 6307840 | tf_op jit(solution)/shard_map/mgts,tmgd->smd/dot_general | solution.py:95
  54.8 2.7 %fusion.41 = f32[8,256,128,4]{2,1,3,0:T(8,128)} fusion(bf16[256,8,128,1]{0,2,3,1:T(8,128)(2,1)S(1)} %bitcast.128, bf16[128,8,4,128]{0,3,2,1:T(8,128)(2,1)S(1)} %bitcast.122), kind=kOutput, calls=%fused_computation.64 | convolution fusion | flops 268435456 | bytes 5767168 | tf_op jit(solution)/shard_map/tmgd,smd->mgts/dot_general | solution.py:90
  57.7 1.6 %copy.60 = f32[256,1024]{1,0:T(8,128)S(1)} copy(f32[256,1024]{0,1:T(8,128)} %bitcast.131) | data formatting | bytes 2097152 | tf_op jit(solution)/shard_map/reshape | solution.py:97
  59.3 8.2 %fusion.11 = f32[8,256,128,1]{1,2,3,0:T(8,128)} fusion(bf16[128,8,4,128]{0,3,2,1:T(8,128)(2,1)S(1)} %bitcast.130, f32[8,256,128,4]{2,1,3,0:T(8,128)} %fusion.41, f32[8,4,128,256]{2,3,1,0:T(8,128)} %get-tuple-element.30, f32[8,4,128]{2,1,0:T(4,128)S(1)} %get-tuple-element.29), kind=kOutput, calls=%fused_computation.19 | convolution fusion | flops 275779840 | bytes 10502144 | tf_op jit(solution)/shard_map/mgts,tmgd->smd/dot_general | solution.py:94
  67.5 1.6 %copy.59 = f32[256,1024]{1,0:T(8,128)S(1)} copy(f32[256,1024]{0,1:T(8,128)} %bitcast.133) | data formatting | bytes 2097152 | tf_op jit(solution)/shard_map/reshape | solution.py:97
  69.9 1.3 collective-permute-start.2
  71.3 11.8 %all_gather.11 = bf16[1024,257]{1,0:T(8,128)(2,1)} all-gather(bf16[128,257]{1,0:T(8,128)(2,1)S(1)} %pad_maximum_fusion.2), channel_id=1, replica_groups=mesh['dp'=8,'seq'=4] {'dp'}, dimensions={0}, use_global_device_ids=true | all-gather | bytes 592128 | tf_op jit(solution)/shard_map/all_gather | solution.py:85
  83.2 2.5 %fusion.42 = f32[512,257]{0,1:T(8,128)} fusion(bf16[1024,512]{1,0:T(8,128)(2,1)S(1)} %bitcast.120, bf16[1024,257]{1,0:T(8,128)(2,1)} %all_gather.11), kind=kOutput, calls=%fused_computation.65 | convolution fusion | flops 269484032 | bytes 2101248 | tf_op jit(solution)/shard_map/dot_general | solution.py:86
  85.7 7.4 %fusion.13 = bf16[8,128,4,128]{3,1,2,0:T(8,128)(2,1)S(1)} fusion(bf16[256,8,128,1]{0,2,3,1:T(8,128)(2,1)} %bitcast.135, f32[8,256,128,4]{2,1,3,0:T(8,128)} %fusion.41, f32[8,4,128,256]{2,3,1,0:T(8,128)} %get-tuple-element.30, f32[8,4,128]{2,1,0:T(4,128)S(1)} %get-tuple-element.29), kind=kOutput, calls=%fused_computation.22 | convolution fusion | flops 276304128 | bytes 9977856 | tf_op jit(solution)/shard_map/mgts,smd->tmgd/dot_general | solution.py:93
  93.0 1.3 copy.63
  94.4 1.1 fusion.17
  96.3 31.2 %all-reduce.3.cloned.1.call-done = f32[512,257]{0,1:T(8,128)} async-done(((f32[512,257]{0,1:T(8,128)}), f32[512,257]{0,1:T(8,128)}) %all-reduce.3.cloned.1.call-update) | async-done | bytes 526352 | tf_op jit(solution)/shard_map/psum | solution.py:87
  129.6 1.3 slice.48
  (47 shorter events, 10.5 us)
Async XLA Ops:
  7.2 38.2 %all-gather.3.cloned.1.call-start = ((), (), s32[]{:S(2)}) async-start(), calls=%async_computation.1 | async-start | bytes 2359296 | tf_op jit(solution)/shard_map/all_gather | solution.py:43
  10.2 21.5 %collective-permute-start = (bf16[128,2048]{0,1:T(8,128)(2,1)S(1)}, bf16[128,2048]{0,1:T(8,128)(2,1)S(1)}, u32[]{:S(2)}, u32[]{:S(2)}) collective-permute-start(bf16[128,2048]{0,1:T(8,128)(2,1)S(1)} %pad_maximum_fusion.1), channel_id=1, source_target_pairs={{0,1},{1,2},{2,3},{4,5},{5,6},{6,7},{8,9},{9,10},{10,11},{12,13},{... | collective-permute-start | bytes 1572872 | tf_op jit(solution)/shard_map/ppermute | solution.py:22
  31.6 3.7 %copy-start.2 = (bf16[1,128,4096]{1,2,0:T(8,128)(2,1)}, bf16[1,128,4096]{1,2,0:T(8,128)(2,1)S(1)}, u32[]{:S(2)}) copy-start(bf16[1,128,4096]{1,2,0:T(8,128)(2,1)S(1)} %copy.79) | copy-start | bytes 3145732
  31.9 3.5 %copy-start.4 = (bf16[256,1024]{0,1:T(8,128)(2,1)}, bf16[256,1024]{0,1:T(8,128)(2,1)S(1)}, u32[]{:S(2)}) copy-start(bf16[256,1024]{0,1:T(8,128)(2,1)S(1)} %get-tuple-element.23) | copy-start | bytes 1572868
  31.9 6.2 %copy-start = (bf16[256,1024]{0,1:T(8,128)(2,1)}, bf16[256,1024]{0,1:T(8,128)(2,1)S(1)}, u32[]{:S(2)}) copy-start(bf16[256,1024]{0,1:T(8,128)(2,1)S(1)} %get-tuple-element.22) | copy-start | bytes 1572868
  38.1 7.3 %copy-start.5 = (s32[1,128]{1,0:T(1,128)S(1)}, s32[1,128]{1,0:T(1,128)}, u32[]{:S(2)}) copy-start(s32[1,128]{1,0:T(1,128)} %param.13) | copy-start | bytes 1540
  38.1 9.5 %copy-start.6 = (s32[1,128]{1,0:T(1,128)S(1)}, s32[1,128]{1,0:T(1,128)}, u32[]{:S(2)}) copy-start(s32[1,128]{1,0:T(1,128)} %param.14) | copy-start | bytes 1540
  38.4 6.3 %collective-permute-start.1 = (f32[1]{0:T(128)S(1)}, f32[1]{0:T(128)}, u32[]{:S(2)}, u32[]{:S(2)}) collective-permute-start(f32[1]{0:T(128)S(1)} %bitcast.142), channel_id=1, source_target_pairs={{1,0},{2,1},{3,2},{5,4},{6,5},{7,6},{9,8},{10,9},{11,10},{13,12},{... | collective-permute-start | bytes 20 | tf_op jit(solution)/shard_map/ppermute | solution.py:22
  41.1 42.1 %all-to-all-start = ((bf16[128,8,512]{2,0,1:T(8,128)(2,1)}), bf16[128,8,512]{2,0,1:T(8,128)(2,1)S(1)}, u32[]{:S(2)}, u32[]{:S(2)}) async-start(bf16[128,8,512]{2,0,1:T(8,128)(2,1)} %copy.61), calls=%async_computation | async-start | bytes 2097152 | tf_op jit(solution)/shard_map/all_to_all | solution.py:70
  44.7 82.8 %all-reduce.3.cloned.1.call-start = ((), (), s32[]{:S(2)}) async-start(), calls=%async_computation.2 | async-start | bytes 1081344 | tf_op jit(solution)/shard_map/psum | solution.py:87
  50.8 4.0 %copy-start.1 = (bf16[256,1024]{0,1:T(8,128)(2,1)S(1)}, bf16[256,1024]{0,1:T(8,128)(2,1)}, u32[]{:S(2)}) copy-start(bf16[256,1024]{0,1:T(8,128)(2,1)} %copy-done) | copy-start | bytes 1572868
  54.8 4.4 %copy-start.3 = (bf16[1,128,4096]{1,2,0:T(8,128)(2,1)S(1)}, bf16[1,128,4096]{1,2,0:T(8,128)(2,1)}, u32[]{:S(2)}) copy-start(bf16[1,128,4096]{1,2,0:T(8,128)(2,1)} %copy-done.2) | copy-start | bytes 3145732
  69.9 24.5 %collective-permute-start.2 = (bf16[128,2048]{1,0:T(8,128)(2,1)}, bf16[128,2048]{1,0:T(8,128)(2,1)}, u32[]{:S(2)}, u32[]{:S(2)}) collective-permute-start(bf16[128,2048]{1,0:T(8,128)(2,1)} %fusion.18), channel_id=1, source_target_pairs={{1,0},{2,1},{3,2},{5,4},{6,5},{7,6},{9,8},{10,9},{11,10},{13,12},{... | collective-permute-start | bytes 1572872 | tf_op jit(solution)/shard_map/ppermute | solution.py:22
Sparse Core Ops, SparseCore 0:
  9.9 30.6 all-gather.2
  85.8 41.6 all-reduce.2
where the time goes:
time: 139 us; the launch traced here: 138 us
  matrix products  35.8 us (26%)
  waiting for transfers between devices  31.9 us (23%)
  blocking collectives  20.7 us (15%)
  between operations  17.6 us (13%)
  local copies, waits for them, and re-layouts  17.4 us (13%)
  starting transfers between devices  11.2 us (8%)
  other arithmetic  3.18 us (2%)
    psum x1, waiting for transfers between devices, per_device(): part = lax.psum(part, 'seq')  31.2 us
    all_gather x1, blocking collectives, per_device(): steer_all = lax.all_gather(steer, 'dp', axis=0, tiled=True)  11.8 us
    all_gather x1, blocking collectives, per_device(): lax.all_gather(value_weight, 'dp', axis=0, tiled=True)  8.89 us
    dot_general x1, matrix products, per_device(): jnp.einsum('mgts,tmgd->smd', d_scores, q_heads, preferred_element_type=jn...  8.18 us
    ppermute x3, starting transfers between devices, passed_along(): return lax.ppermute(x, axis, pairs)  7.54 us
    dot_general x1, matrix products, per_device(): jnp.einsum('mgts,smd->tmgd', d_scores, k_heads, preferred_element_type=jn...  7.37 us
    unnamed x20, local copies, waits for them, and re-layouts  5.28 us
    dot_general x1, matrix products, per_device(): jnp.einsum('mgts,tmgd->smd', probs_low, d_heads, preferred_element_type=j...  4.02 us
  transfers between devices with their start and end apart: 6, of which 1 were waited for; matrix products, arithmetic and copies ran while one was open for 38% of the time, Pallas kernels for 0%

commit v1 on v0

v1 whole, which is shorter than its diff:
```python
import functools

import jax
import jax.numpy as jnp
from jax import lax
from jax.experimental import pallas as pl
from jax.experimental.pallas import tpu as pltpu
from jax.sharding import PartitionSpec as P

HEADS = 32
KV_HEADS = 8
HD = 128
ACTS = 256
BLOCK = 128
GROUP = HEADS // KV_HEADS
GW = GROUP * HD

GAMMA = 0.99
TAU = 0.7
REWARD_UNIT = 64.0
NEG_FILL = -1e30
SCALE = HD ** (-0.5)

F32 = jnp.float32
BF16 = jnp.bfloat16
MESH = pl.DeviceIdType.MESH

NT = (((1,), (1,)), ((), ()))
NN = (((1,), (0,)), ((), ()))
TN = (((0,), (0,)), ((), ()))


def mul(a, b, dims):
    return lax.dot_general(a, b, dims, preferred_element_type=F32)


def stacked(x):
    return jnp.concatenate([x[:, i * HD : (i + 1) * HD] for i in range(GROUP)], axis=0)


def side_by_side(x):
    return jnp.concatenate([x[i * BLOCK : (i + 1) * BLOCK] for i in range(GROUP)], axis=1)


def kernel(
    D, S, FL,
    q_ref, k_ref, v_ref, hw_ref, vw_ref, act_ref, rew_ref, ep_ref,
    dq_ref, dk_ref, dv_ref, gh_ref, gv_ref,
    kprev, vprev, hw_all, vw_all, bias, probs, att, shared, q_acc, v_acc, v_out, v_in,
    sel, gvb, steer, sel_t, dks, dvs, dkr, dvr, dka, dva, part, pre_in, pre_out, suf_in, suf_out,
    k_s, k_r, v_s, v_r, hw_s, hw_f, hw_r, vw_s, vw_r, at_s, at_r, st_s, st_r, vn_s, vn_r,
    dk_s, dk_r, dv_s, dv_r, pre_s, pre_r, suf_s, suf_r,
):
    dp = lax.axis_index("dp")
    sq = lax.axis_index("seq")
    sib = dp + 1 - 2 * (dp % 2)
    R = GW // FL
    rows = ACTS + 16
    cuts = ((0, 128), (128, rows - 128))

    def copy(src, dst, ss, rs, where):
        return pltpu.make_async_remote_copy(
            src_ref=src, dst_ref=dst, send_sem=ss, recv_sem=rs, device_id=where, device_id_type=MESH
        )

    def order(j):
        if R == 1:
            return (dp + j - 2 * (dp % 2) * (j % 2) + D) % D
        return (dp // R + j) % KV_HEADS

    def lanes(i, width):
        return pl.ds(pl.multiple_of(i * width, width), width)

    def k_copy(g):
        return copy(k_ref.at[:, lanes(g, HD)], kprev.at[:, lanes(g, HD)], k_s.at[g], k_r.at[g], {"seq": sq + 1})

    def v_copy(g):
        return copy(v_ref.at[:, lanes(g, HD)], vprev.at[:, lanes(g, HD)], v_s.at[g], v_r.at[g], {"seq": sq + 1})

    def hw_copy(p):
        return copy(hw_ref, hw_all.at[lanes(dp, FL), :], hw_s.at[p], hw_r.at[dp], {"dp": p})

    def hw_own(_):
        return copy(hw_ref, hw_all.at[lanes(dp, FL), :], hw_f.at[dp], hw_r.at[dp], {"dp": sib})

    def hw_pass(o):
        return copy(hw_all.at[lanes(o, FL), :], hw_all.at[lanes(o, FL), :], hw_f.at[o], hw_r.at[o], {"dp": sib})

    def vw_copy(p):
        return copy(vw_ref, vw_all.at[lanes(dp, 16), :], vw_s.at[p], vw_r.at[dp], {"dp": p})

    def vw_got(p):
        return copy(vw_ref, vw_all.at[lanes(p, 16), :], vw_s.at[p], vw_r.at[p], {"dp": p})

    def at_copy(o):
        return copy(att.at[:, lanes(o, FL)], shared.at[lanes(dp, BLOCK), :], at_s.at[o], at_r.at[dp], {"dp": o})

    def at_got(p):
        return copy(att.at[:, lanes(p, FL)], shared.at[lanes(p, BLOCK), :], at_s.at[p], at_r.at[p], {"dp": p})

    def st_copy(p):
        return copy(steer.at[lanes(dp, 8), :], steer.at[lanes(dp, 8), :], st_s.at[p], st_r.at[dp], {"dp": p})

    def st_got(p):
        return copy(steer.at[lanes(p, 8), :], steer.at[lanes(p, 8), :], st_s.at[p], st_r.at[p], {"dp": p})

    def vn_copy():
        return copy(v_out, v_in, vn_s.at[0], vn_r.at[0], {"seq": sq - 1})

    def dk_copy(g):
        return copy(dks.at[:, lanes(g, HD)], dkr.at[:, lanes(g, HD)], dk_s.at[g], dk_r.at[g], {"seq": sq - 1})

    def dv_copy(g):
        return copy(dvs.at[:, lanes(g, HD)], dvr.at[:, lanes(g, HD)], dv_s.at[g], dv_r.at[g], {"seq": sq - 1})

    def pre_copy(c):
        w = pl.ds(*cuts[c])
        return copy(pre_out.at[w, :], pre_in.at[w, :], pre_s.at[c], pre_r.at[c], {"seq": sq + 1})

    def suf_copy(c):
        w = pl.ds(*cuts[c])
        return copy(suf_out.at[w, :], suf_in.at[w, :], suf_s.at[c], suf_r.at[c], {"seq": sq - 1})

    def loop(low, high, body):
        def step(i, carry):
            body(i)
            return carry

        lax.fori_loop(low, high, step, 0)

    has_left, has_right = sq > 0, sq < S - 1

    barrier = pltpu.get_barrier_semaphore()

    @functools.partial(loop, 1, D)
    def _(m):
        pl.semaphore_signal(barrier, inc=1, device_id={"dp": (dp + m) % D}, device_id_type=MESH)

    @pl.when(has_left)
    def _():
        pl.semaphore_signal(barrier, inc=1, device_id={"seq": sq - 1}, device_id_type=MESH)

    @pl.when(has_right)
    def _():
        pl.semaphore_signal(barrier, inc=1, device_id={"seq": sq + 1}, device_id_type=MESH)

    pl.semaphore_wait(barrier, D - 1 + jnp.where(has_left, 1, 0) + jnp.where(has_right, 1, 0))

    @pl.when(has_right)
    def _():
        @functools.partial(loop, 0, KV_HEADS)
        def _(j):
            g = order(j)
            k_copy(g).start()
            v_copy(g).start()

    hw_own(0).start()

    @functools.partial(loop, 1, D // 2)
    def _(m):
        hw_copy((dp + D - 2 * m) % D).start()

    @functools.partial(loop, 1, D)
    def _(m):
        vw_copy((dp + m) % D).start()

    hw_all[lanes(dp, FL), :] = hw_ref[...]
    vw_all[lanes(dp, 16), :] = vw_ref[...]

    @pl.when(sq == 0)
    def _():
        kprev[...] = jnp.zeros_like(kprev)
        vprev[...] = jnp.zeros_like(vprev)
        pre_in[...] = jnp.zeros_like(pre_in)

    @pl.when(sq == S - 1)
    def _():
        dkr[...] = jnp.zeros_like(dkr)
        dvr[...] = jnp.zeros_like(dvr)
        v_in[...] = jnp.zeros_like(v_in)
        suf_in[...] = jnp.zeros_like(suf_in)

    mine = ep_ref[0, sq]
    left_ep = jnp.where(has_left, ep_ref[0, jnp.maximum(sq - 1, 0)], -1)
    right_ep = jnp.where(has_right, ep_ref[0, jnp.minimum(sq + 1, S - 1)], -1)
    key_at = lax.broadcasted_iota(jnp.int32, (BLOCK, BLOCK), 0)
    query_at = lax.broadcasted_iota(jnp.int32, (BLOCK, BLOCK), 1)
    mine_v = jnp.full((BLOCK, BLOCK), mine, jnp.int32)
    bias[:BLOCK, :] = jnp.where(mine_v == jnp.full((BLOCK, BLOCK), left_ep, jnp.int32), 0.0, NEG_FILL)
    bias[BLOCK:, :] = jnp.where(key_at <= query_at, 0.0, NEG_FILL)
    q_acc[...] = jnp.zeros_like(q_acc)
    v_acc[...] = jnp.zeros_like(v_acc)

    @functools.partial(loop, 1, D)
    def _(m):
        vw_got((dp + m) % D).wait_recv()

    def value_row(g):
        if R == 1:
            return vw_all[lanes(g, 16), :][0:1, :].astype(F32)
        return jnp.concatenate(
            [vw_all[lanes(g * R + r, 16), :][0:1, :].astype(F32) for r in range(R)], axis=1
        )

    def pair(prev, own, g):
        return jnp.concatenate([prev[:, lanes(g, HD)], own[:, lanes(g, HD)]], axis=0)

    @functools.partial(loop, 0, KV_HEADS)
    def _(j):
        g = order(j)

        @pl.when(has_left)
        def _():
            k_copy(g).wait_recv()
            v_copy(g).wait_recv()

        s = mul(pair(kprev, k_ref, g), stacked(q_ref[:, lanes(g, GW)]), NT) * SCALE
        s = s + jnp.concatenate([bias[...]] * GROUP, axis=1)
        e = jnp.exp(s - jnp.max(s, axis=0, keepdims=True))
        p = (e * (1.0 / jnp.sum(e, axis=0, keepdims=True))).astype(BF16)
        probs[g] = p
        a = side_by_side(mul(p, pair(vprev, v_ref, g), TN)).astype(BF16)
        att[:, lanes(g, GW)] = a
        for r in range(R):
            o = g * R + r

            @pl.when(o != dp)
            def _():
                at_copy(o).start()

            @pl.when(o == dp)
            def _():
                shared[lanes(dp, BLOCK), :] = att[:, lanes(o, FL)]

        for r in range(R):
            o = g * R + r

            @pl.when(jnp.logical_and(o != dp, o % 2 == dp % 2))
            def _():
                hw_pass(o).wait_recv()
                hw_pass(o).start()

        for r in range(R):
            o = g * R + r

            @pl.when(o % 2 != dp % 2)
            def _():
                hw_pass(o).wait_recv()

        q_acc[...] += mul(a, hw_all[lanes(g, GW), :], NN)
        weighed = a.astype(F32) * value_row(g)
        v_acc[...] += sum(weighed[:, i * HD : (i + 1) * HD] for i in range(GROUP))

    wide = (BLOCK, BLOCK)
    act_row = act_ref[...].astype(F32)
    act_b = jnp.broadcast_to(act_row, wide).T
    rew_b = jnp.broadcast_to(rew_ref[...].astype(F32), wide).T
    hot = jnp.concatenate([act_b, act_b], axis=1) == lax.broadcasted_iota(
        jnp.int32, (BLOCK, ACTS), 1
    ).astype(F32)
    v_now = jnp.broadcast_to(jnp.sum(v_acc[...], axis=1, keepdims=True), wide)
    v_out[...] = v_now[:8]

    @pl.when(has_left)
    def _():
        vn_copy().start()

    q_taken = jnp.broadcast_to(
        jnp.sum(jnp.where(hot, q_acc[...], 0.0), axis=1, keepdims=True), wide
    )

    @pl.when(has_right)
    def _():
        vn_copy().wait_recv()

    after = jnp.where(
        mine_v == jnp.full(wide, right_ep, jnp.int32), jnp.broadcast_to(v_in[0:1, :], wide), 0.0
    )
    v_next = jnp.where(key_at == BLOCK - 1, after, pltpu.roll(v_now, BLOCK - 1, 0))
    err = q_taken - (rew_b / REWARD_UNIT + GAMMA * v_next)
    gap = q_taken - v_now
    weight = jnp.where(gap < 0, 1.0 - TAU, TAU)
    grad_q = (2.0 * err).astype(BF16).astype(F32)
    grad_v = (-2.0 * weight * gap).astype(BF16).astype(F32)
    gvb[...] = grad_v
    sel[...] = jnp.where(hot, jnp.concatenate([grad_q, grad_q], axis=1), 0.0).astype(BF16)
    steer[lanes(dp, 8), :] = jnp.concatenate(
        [grad_q.T[0:1], grad_v.T[0:1], act_row, jnp.zeros((5, BLOCK), F32)], axis=0
    )

    @functools.partial(loop, 1, D)
    def _(m):
        st_copy((dp + m) % D).start()

    def backward(j):
        g = order(j)
        v_row = value_row(g)
        d = mul(sel[...], hw_all[lanes(g, GW), :], NT)
        d = (d + jnp.concatenate([gvb[...]] * GROUP, axis=1) * v_row).astype(BF16)
        d4 = stacked(d)
        p_low = probs[g]
        p = p_low.astype(F32)
        d_p = mul(pair(vprev, v_ref, g), d4, NT)
        delta = jnp.sum(p * d_p, axis=0, keepdims=True)
        d_s = (p * (d_p - delta) * SCALE).astype(BF16)
        dk = mul(d_s, stacked(q_ref[:, lanes(g, GW)]), NN)
        dv = mul(p_low, d4, NN)
        dks[:, lanes(g, HD)] = dk[:BLOCK].astype(BF16)
        dvs[:, lanes(g, HD)] = dv[:BLOCK].astype(BF16)

        @pl.when(has_left)
        def _():
            dk_copy(g).start()
            dv_copy(g).start()

        dka[:, lanes(g, HD)] = dk[BLOCK:]
        dva[:, lanes(g, HD)] = dv[BLOCK:]
        dq_ref[:, lanes(g, GW)] = side_by_side(mul(d_s, pair(kprev, k_ref, g), TN)).astype(BF16)

    def head_part():
        @functools.partial(loop, 1, D)
        def _(m):
            st_got((dp + m) % D).wait_recv()
            at_got((dp + m) % D).wait_recv()

        act_at = lax.broadcasted_iota(jnp.int32, (ACTS, BLOCK), 0).astype(F32)
        for r in range(D):
            w = pl.ds(r * BLOCK, BLOCK)
            one = steer[pl.ds(r * 8, 8), :]
            sel_t[:ACTS, w] = jnp.where(act_at == one[2:3], one[0:1], 0.0).astype(BF16)
            sel_t[ACTS:, w] = jnp.broadcast_to(one[1:2], (16, BLOCK)).astype(BF16)
        part[...] = mul(sel_t[...], shared[...], NN)

    def stage(k):
        @pl.when(sq == k)
        def _():
            for c, (low, size) in enumerate(cuts):
                if k > 0:
                    pre_copy(c).wait_recv()
                w = pl.ds(low, size)
                pre_out[w, :] = (part[w, :] + pre_in[w, :].astype(F32)).astype(BF16)
                pre_copy(c).start()

        @pl.when(sq == S - 1 - k)
        def _():
            for c, (low, size) in enumerate(cuts):
                if k > 0:
                    suf_copy(c).wait_recv()
                w = pl.ds(low, size)
                suf_out[w, :] = (part[w, :] + suf_in[w, :].astype(F32)).astype(BF16)
                suf_copy(c).start()

    for half in range(4):
        loop(2 * half, 2 * half + 2, backward)
        if half == 0:
            head_part()
        if half < S - 1:
            stage(half)
    for k in range(4, S - 1):
        stage(k)

    @functools.partial(loop, 0, KV_HEADS)
    def _(j):
        g = order(j)

        @pl.when(has_right)
        def _():
            dk_copy(g).wait_recv()
            dv_copy(g).wait_recv()

        w = lanes(g, HD)
        dk_ref[:, w] = (dka[:, w] + dkr[:, w].astype(F32)).astype(BF16)
        dv_ref[:, w] = (dva[:, w] + dvr[:, w].astype(F32)).astype(BF16)

    @pl.when(sq == S - 1)
    def _():
        for c in range(len(cuts)):
            pre_copy(c).wait_recv()

    @pl.when(sq == 0)
    def _():
        for c in range(len(cuts)):
            suf_copy(c).wait_recv()

    total = part[...] + pre_in[...].astype(F32) + suf_in[...].astype(F32)
    gh_ref[...] = total[:ACTS].T
    gv_ref[...] = total[ACTS : ACTS + 8]

    @pl.when(has_right)
    def _():
        @functools.partial(loop, 0, KV_HEADS)
        def _(g):
            k_copy(g).wait_send()
            v_copy(g).wait_send()

        for c in range(len(cuts)):
            pre_copy(c).wait_send()

    @pl.when(has_left)
    def _():
        @functools.partial(loop, 0, KV_HEADS)
        def _(g):
            dk_copy(g).wait_send()
            dv_copy(g).wait_send()

        vn_copy().wait_send()
        for c in range(len(cuts)):
            suf_copy(c).wait_send()

    hw_own(0).wait_send()

    @functools.partial(loop, 1, D // 2)
    def _(m):
        hw_copy((dp + D - 2 * m) % D).wait_send()
        hw_pass((dp + 2 * m) % D).wait_send()

    @functools.partial(loop, 1, D)
    def _(m):
        p = (dp + m) % D
        vw_copy(p).wait_send()
        at_copy(p).wait_send()
        st_copy(p).wait_send()


def per_device(D, S, queries, keys, values, head_weight, value_weight, action_ids, rewards, episode_ids):
    FL = head_weight.shape[0]
    qw, kw = HEADS * HD, KV_HEADS * HD
    rows = ACTS + 16
    dma = lambda n: pltpu.SemaphoreType.DMA((n,))
    vm = pltpu.VMEM
    vmem = pl.BlockSpec(memory_space=pltpu.VMEM)
    values_row = jnp.broadcast_to(value_weight[None], (16, FL))
    outs = pl.pallas_call(
        functools.partial(kernel, D, S, FL),
        out_shape=(
            jax.ShapeDtypeStruct((BLOCK, qw), BF16),
            jax.ShapeDtypeStruct((BLOCK, kw), BF16),
            jax.ShapeDtypeStruct((BLOCK, kw), BF16),
            jax.ShapeDtypeStruct((FL, ACTS), F32),
            jax.ShapeDtypeStruct((8, FL), F32),
        ),
        in_specs=[vmem] * 7 + [pl.BlockSpec(memory_space=pltpu.SMEM)],
        out_specs=(vmem,) * 5,
        scratch_shapes=[
            vm((BLOCK, kw), BF16), vm((BLOCK, kw), BF16),
            vm((qw, ACTS), BF16), vm((D * 16, FL), BF16),
            vm((2 * BLOCK, BLOCK), F32), vm((KV_HEADS, 2 * BLOCK, GW), BF16),
            vm((BLOCK, qw), BF16), vm((D * BLOCK, FL), BF16),
            vm((BLOCK, ACTS), F32), vm((BLOCK, BLOCK), F32),
            vm((8, BLOCK), F32), vm((8, BLOCK), F32),
            vm((BLOCK, ACTS), BF16), vm((BLOCK, BLOCK), F32), vm((D * 8, BLOCK), F32),
            vm((rows, D * BLOCK), BF16),
            vm((BLOCK, kw), BF16), vm((BLOCK, kw), BF16),
            vm((BLOCK, kw), BF16), vm((BLOCK, kw), BF16),
            vm((BLOCK, kw), F32), vm((BLOCK, kw), F32),
            vm((rows, FL), F32),
            vm((rows, FL), BF16), vm((rows, FL), BF16), vm((rows, FL), BF16), vm((rows, FL), BF16),
            dma(KV_HEADS), dma(KV_HEADS), dma(KV_HEADS), dma(KV_HEADS),
            dma(D), dma(D), dma(D), dma(D), dma(D), dma(D), dma(D), dma(D), dma(D),
            dma(1), dma(1),
            dma(KV_HEADS), dma(KV_HEADS), dma(KV_HEADS), dma(KV_HEADS),
            dma(2), dma(2), dma(2), dma(2),
        ],
        compiler_params=pltpu.CompilerParams(
            collective_id=0, has_side_effects=True, vmem_limit_bytes=48 * 2**20
        ),
    )(queries[0], keys[0], values[0], head_weight, values_row, action_ids, rewards, episode_ids)
    dq, dk, dv, gh, gv = outs
    return (dq[None], dk[None], dv[None], gh, gv[0])


def solution(mesh):
    return jax.shard_map(
        functools.partial(per_device, mesh.shape["dp"], mesh.shape["seq"]),
        mesh=mesh,
        in_specs=(
            P("dp", "seq", None),
            P("dp", "seq", None),
            P("dp", "seq", None),
            P("dp", None),
            P("dp"),
            P("dp", "seq"),
            P("dp", "seq"),
            P("dp", None),
        ),
        out_specs=(
            P("dp", "seq", None),
            P("dp", "seq", None),
            P("dp", "seq", None),
            P("dp", None),
            P("dp"),
        ),
        check_vma=False,
    )
```

time: 139 us -> 70.3 us (0.51)
  Pallas kernels: 0 us -> 60.2 us
  matrix products: 35.8 us -> 0 us
  waiting for transfers between devices: 31.9 us -> 0 us
  blocking collectives: 20.7 us -> 0 us
  between operations: 17.6 us -> 0.66 us
  starting transfers between devices: 11.2 us -> 0 us
  local copies, waits for them, and re-layouts: 17.4 us -> 9.17 us
  other arithmetic: 3.18 us -> 0 us
    pallas_call x0 -> x1, Pallas kernels: none -> 60.2 us  [per_device(): pl.pallas_call(functools.partial(kernel, D, S, FL), out_shape=(jax.ShapeD...]
    dot_general x9 -> x0, matrix products: 32.4 us -> none  [the longest x1 8.18 us: per_device(): jnp.einsum('mgts,tmgd->smd', d_scores, q_heads, preferred_element_type=jn...]
    psum x1 -> x0, waiting for transfers between devices: 31.2 us -> none  [per_device(): part = lax.psum(part, 'seq')]
    all_gather x2 -> x0, blocking collectives: 20.7 us -> none  [the longest x1 11.8 us: per_device(): steer_all = lax.all_gather(steer, 'dp', axis=0, tiled=True)]
    ppermute x3 -> x0, starting transfers between devices: 7.54 us -> none  [passed_along(): return lax.ppermute(x, axis, pairs)]
    reshape x3 -> x0, local copies, waits for them, and re-layouts: 3.77 us -> none  [the longest x1 1.56 us: per_device(): value_sum.reshape(2 * tok_local, width)]
    all_to_all x1 -> x0, starting transfers between devices: 3.56 us -> none  [per_device(): lax.all_to_all(attended, 'dp', split_axis=1, concat_axis=0, tiled=True)]
    sub x1 -> x0, matrix products: 3.43 us -> none  [per_device(): expo = jnp.exp(scores - top)]
  transfers between devices with their start and end apart: 6 -> 0, of which waited for: 1 -> 0; matrix products, arithmetic and copies ran while one was open for 38% -> 0% of each run, Pallas kernels for 0% -> 0%
where the time goes in v1:
time: 70.3 us; the launch traced here: 70 us
  Pallas kernels  60.2 us (86%)
  local copies, waits for them, and re-layouts  9.17 us (13%)
    pallas_call x1, Pallas kernels, per_device(): pl.pallas_call(functools.partial(kernel, D, S, FL), out_shape=(jax.ShapeD...  60.2 us
    unnamed x20, local copies, waits for them, and re-layouts  8.59 us

profile of v1, /device:TPU:0, one launch (start us, length us, event | category | flops | bytes accessed | tf_op | source)
XLA Modules:
  0.0 70.0 jit_solution(7348171731078503313)
XLA Ops:
  0.6 0.0 copy-start.7
  0.6 0.7 copy-done.7
  1.3 0.0 copy-start.4
  1.3 0.0 copy-start.5
  1.3 0.0 copy-start.6
  1.3 0.6 copy-done.4
  2.0 0.0 copy-done.5
  2.0 0.0 copy-done.6
  2.0 0.0 copy-start
  2.0 1.2 %copy-done = bf16[1,128,4096]{2,1,0:T(8,128)(2,1)S(1)} copy-done((bf16[1,128,4096]{2,1,0:T(8,128)(2,1)S(1)}, bf16[1,128,4096]{2,1,0:T(8,128)(2,1)}, u32[]{:S(2)}) %copy-start) | copy-done | bytes 1048600
  3.2 0.0 copy-start.1
  3.2 0.9 %copy-done.1 = bf16[1,128,1024]{2,1,0:T(8,128)(2,1)S(1)} copy-done((bf16[1,128,1024]{2,1,0:T(8,128)(2,1)S(1)}, bf16[1,128,1024]{2,1,0:T(8,128)(2,1)}, u32[]{:S(2)}) %copy-start.1) | copy-done | bytes 262168
  4.2 0.0 copy-start.2
  4.2 0.9 %copy-done.2 = bf16[1,128,1024]{2,1,0:T(8,128)(2,1)S(1)} copy-done((bf16[1,128,1024]{2,1,0:T(8,128)(2,1)S(1)}, bf16[1,128,1024]{2,1,0:T(8,128)(2,1)}, u32[]{:S(2)}) %copy-start.2) | copy-done | bytes 262168
  5.1 0.0 copy-start.3
  5.1 0.9 %copy-done.3 = bf16[512,256]{1,0:T(8,128)(2,1)S(1)} copy-done((bf16[512,256]{1,0:T(8,128)(2,1)S(1)}, bf16[512,256]{1,0:T(8,128)(2,1)}, u32[]{:S(2)}) %copy-start.3) | copy-done | bytes 262168
  6.1 60.2 %shard_map.119 = (bf16[128,4096]{1,0:T(8,128)(2,1)S(1)}, bf16[128,1024]{1,0:T(8,128)(2,1)S(1)}, bf16[128,1024]{1,0:T(8,128)(2,1)S(1)}, f32[512,256]{1,0:T(8,128)S(1)}, f32[8,512]{1,0:T(8,128)S(1)}) custom-call(bf16[128,4096]{1,0:T(8,128)(2,1)S(1)} %bitcast.7, bf16[128,1024]{1,0:T(8,128)(2,1)S(1)} %bitcast.11, bf16[128,1024]{1,0:T(8,128)(2,1)S(1)} %bitcast.12, ...), custom_call_target="tpu_custom_call" | custom-call | tf_op jit(solution)/shard_map/pallas_call | solution.py:433
  66.3 0.6 slice.3
  66.8 1.0 %copy.17 = bf16[1,128,4096]{2,1,0:T(8,128)(2,1)} copy(bf16[1,128,4096]{2,1,0:T(8,128)(2,1)S(1)} %bitcast.8) | data formatting | bytes 2097152
  67.8 0.7 %copy.18 = bf16[1,128,1024]{2,1,0:T(8,128)(2,1)} copy(bf16[1,128,1024]{2,1,0:T(8,128)(2,1)S(1)} %bitcast.10) | data formatting | bytes 524288
  68.5 0.7 %copy.19 = bf16[1,128,1024]{2,1,0:T(8,128)(2,1)} copy(bf16[1,128,1024]{2,1,0:T(8,128)(2,1)S(1)} %bitcast.9) | data formatting | bytes 524288
  69.2 0.8 %copy.20 = f32[512,256]{1,0:T(8,128)} copy(f32[512,256]{1,0:T(8,128)S(1)} %get-tuple-element.23) | data formatting | bytes 1048576
  (1 shorter events, 0.0 us)
Async XLA Ops:
  0.6 0.7 copy-start.7
  1.3 0.7 copy-start.4
  1.3 0.7 copy-start.5
  1.3 0.7 copy-start.6
  2.0 1.2 %copy-start = (bf16[1,128,4096]{2,1,0:T(8,128)(2,1)S(1)}, bf16[1,128,4096]{2,1,0:T(8,128)(2,1)}, u32[]{:S(2)}) copy-start(bf16[1,128,4096]{2,1,0:T(8,128)(2,1)} %param.8) | copy-start | bytes 3145732
  3.2 0.9 %copy-start.1 = (bf16[1,128,1024]{2,1,0:T(8,128)(2,1)S(1)}, bf16[1,128,1024]{2,1,0:T(8,128)(2,1)}, u32[]{:S(2)}) copy-start(bf16[1,128,1024]{2,1,0:T(8,128)(2,1)} %param.9) | copy-start | bytes 786436
  4.2 0.9 %copy-start.2 = (bf16[1,128,1024]{2,1,0:T(8,128)(2,1)S(1)}, bf16[1,128,1024]{2,1,0:T(8,128)(2,1)}, u32[]{:S(2)}) copy-start(bf16[1,128,1024]{2,1,0:T(8,128)(2,1)} %param.10) | copy-start | bytes 786436
  5.1 0.9 %copy-start.3 = (bf16[512,256]{1,0:T(8,128)(2,1)S(1)}, bf16[512,256]{1,0:T(8,128)(2,1)}, u32[]{:S(2)}) copy-start(bf16[512,256]{1,0:T(8,128)(2,1)} %hw_ref.1) | copy-start | bytes 786436

commit v2 on v1

--- a/solution.py
+++ b/solution.py
@@ -44,9 +44,9 @@
 
 def kernel(
     D, S, FL,
-    q_ref, k_ref, v_ref, hw_ref, vw_ref, act_ref, rew_ref, ep_ref,
+    q_hbm, k_hbm, v_hbm, hw_ref, vw_ref, act_ref, rew_ref, ep_ref,
     dq_ref, dk_ref, dv_ref, gh_ref, gv_ref,
-    kprev, vprev, hw_all, vw_all, bias, probs, att, shared, q_acc, v_acc, v_out, v_in,
+    q_ref, k_ref, v_ref, in_sem, kprev, vprev, hw_all, vw_all, bias, probs, att, shared, q_acc, v_acc, v_out, v_in,
     sel, gvb, steer, sel_t, dks, dvs, dkr, dvr, dka, dva, part, pre_in, pre_out, suf_in, suf_out,
     k_s, k_r, v_s, v_r, hw_s, hw_f, hw_r, vw_s, vw_r, at_s, at_r, st_s, st_r, vn_s, vn_r,
     dk_s, dk_r, dv_s, dv_r, pre_s, pre_r, suf_s, suf_r,
@@ -56,7 +56,7 @@
     sib = dp + 1 - 2 * (dp % 2)
     R = GW // FL
     rows = ACTS + 16
-    cuts = ((0, 128), (128, rows - 128))
+    cuts = tuple((32 * c, 32) for c in range(7)) + ((224, rows - 224),)
 
     def copy(src, dst, ss, rs, where):
         return pltpu.make_async_remote_copy(
@@ -72,10 +72,10 @@
         return pl.ds(pl.multiple_of(i * width, width), width)
 
     def k_copy(g):
-        return copy(k_ref.at[:, lanes(g, HD)], kprev.at[:, lanes(g, HD)], k_s.at[g], k_r.at[g], {"seq": sq + 1})
+        return copy(k_hbm.at[:, lanes(g, HD)], kprev.at[g], k_s.at[g], k_r.at[g], {"seq": sq + 1})
 
     def v_copy(g):
-        return copy(v_ref.at[:, lanes(g, HD)], vprev.at[:, lanes(g, HD)], v_s.at[g], v_r.at[g], {"seq": sq + 1})
+        return copy(v_hbm.at[:, lanes(g, HD)], vprev.at[g], v_s.at[g], v_r.at[g], {"seq": sq + 1})
 
     def hw_copy(p):
         return copy(hw_ref, hw_all.at[lanes(dp, FL), :], hw_s.at[p], hw_r.at[dp], {"dp": p})
@@ -108,10 +108,10 @@
         return copy(v_out, v_in, vn_s.at[0], vn_r.at[0], {"seq": sq - 1})
 
     def dk_copy(g):
-        return copy(dks.at[:, lanes(g, HD)], dkr.at[:, lanes(g, HD)], dk_s.at[g], dk_r.at[g], {"seq": sq - 1})
+        return copy(dks.at[g], dkr.at[g], dk_s.at[g], dk_r.at[g], {"seq": sq - 1})
 
     def dv_copy(g):
-        return copy(dvs.at[:, lanes(g, HD)], dvr.at[:, lanes(g, HD)], dv_s.at[g], dv_r.at[g], {"seq": sq - 1})
+        return copy(dvs.at[g], dvr.at[g], dv_s.at[g], dv_r.at[g], {"seq": sq - 1})
 
     def pre_copy(c):
         w = pl.ds(*cuts[c])
@@ -129,6 +129,13 @@
         lax.fori_loop(low, high, step, 0)
 
     has_left, has_right = sq > 0, sq < S - 1
+
+    own = [
+        pltpu.make_async_copy(k_hbm, k_ref, in_sem.at[0]),
+        pltpu.make_async_copy(v_hbm, v_ref, in_sem.at[1]),
+        pltpu.make_async_copy(q_hbm, q_ref, in_sem.at[2]),
+        pltpu.make_async_copy(hw_ref, hw_all.at[lanes(dp, FL), :], in_sem.at[3]),
+    ]
 
     barrier = pltpu.get_barrier_semaphore()
 
@@ -154,17 +161,18 @@
             k_copy(g).start()
             v_copy(g).start()
 
+    @functools.partial(loop, 1, D)
+    def _(m):
+        vw_copy((dp + m) % D).start()
+
     hw_own(0).start()
 
     @functools.partial(loop, 1, D // 2)
     def _(m):
         hw_copy((dp + D - 2 * m) % D).start()
 
-    @functools.partial(loop, 1, D)
-    def _(m):
-        vw_copy((dp + m) % D).start()
-
-    hw_all[lanes(dp, FL), :] = hw_ref[...]
+    for one in own:
+        one.start()
     vw_all[lanes(dp, 16), :] = vw_ref[...]
 
     @pl.when(sq == 0)
@@ -188,12 +196,19 @@
     mine_v = jnp.full((BLOCK, BLOCK), mine, jnp.int32)
     bias[:BLOCK, :] = jnp.where(mine_v == jnp.full((BLOCK, BLOCK), left_ep, jnp.int32), 0.0, NEG_FILL)
     bias[BLOCK:, :] = jnp.where(key_at <= query_at, 0.0, NEG_FILL)
+    for one in own:
+        one.wait()
     q_acc[...] = jnp.zeros_like(q_acc)
     v_acc[...] = jnp.zeros_like(v_acc)
 
     @functools.partial(loop, 1, D)
     def _(m):
         vw_got((dp + m) % D).wait_recv()
+
+    def pass_on(m):
+        o = (dp + 2 * m) % D
+        hw_pass(o).wait_recv()
+        hw_pass(o).start()
 
     def value_row(g):
         if R == 1:
@@ -203,7 +218,7 @@
         )
 
     def pair(prev, own, g):
-        return jnp.concatenate([prev[:, lanes(g, HD)], own[:, lanes(g, HD)]], axis=0)
+        return jnp.concatenate([prev[g], own[:, lanes(g, HD)]], axis=0)
 
     @functools.partial(loop, 0, KV_HEADS)
     def _(j):
@@ -232,14 +247,20 @@
             def _():
                 shared[lanes(dp, BLOCK), :] = att[:, lanes(o, FL)]
 
-        for r in range(R):
-            o = g * R + r
-
-            @pl.when(jnp.logical_and(o != dp, o % 2 == dp % 2))
-            def _():
-                hw_pass(o).wait_recv()
-                hw_pass(o).start()
-
+        @pl.when(jnp.logical_and(j >= 5, j - 4 < D // 2))
+        def _():
+            pass_on(j - 4)
+
+        weighed = a.astype(F32) * value_row(g)
+        v_acc[...] += sum(weighed[:, i * HD : (i + 1) * HD] for i in range(GROUP))
+
+    @functools.partial(loop, 4, D // 2)
+    def _(m):
+        pass_on(m)
+
+    @functools.partial(loop, 0, KV_HEADS)
+    def _(j):
+        g = order(j)
         for r in range(R):
             o = g * R + r
 
@@ -247,9 +268,7 @@
             def _():
                 hw_pass(o).wait_recv()
 
-        q_acc[...] += mul(a, hw_all[lanes(g, GW), :], NN)
-        weighed = a.astype(F32) * value_row(g)
-        v_acc[...] += sum(weighed[:, i * HD : (i + 1) * HD] for i in range(GROUP))
+        q_acc[...] += mul(att[:, lanes(g, GW)], hw_all[lanes(g, GW), :], NN)
 
     wide = (BLOCK, BLOCK)
     act_row = act_ref[...].astype(F32)
@@ -305,8 +324,8 @@
         d_s = (p * (d_p - delta) * SCALE).astype(BF16)
         dk = mul(d_s, stacked(q_ref[:, lanes(g, GW)]), NN)
         dv = mul(p_low, d4, NN)
-        dks[:, lanes(g, HD)] = dk[:BLOCK].astype(BF16)
-        dvs[:, lanes(g, HD)] = dv[:BLOCK].astype(BF16)
+        dks[g] = dk[:BLOCK].astype(BF16)
+        dvs[g] = dv[:BLOCK].astype(BF16)
 
         @pl.when(has_left)
         def _():
@@ -331,33 +350,45 @@
             sel_t[ACTS:, w] = jnp.broadcast_to(one[1:2], (16, BLOCK)).astype(BF16)
         part[...] = mul(sel_t[...], shared[...], NN)
 
-    def stage(k):
-        @pl.when(sq == k)
-        def _():
-            for c, (low, size) in enumerate(cuts):
-                if k > 0:
-                    pre_copy(c).wait_recv()
-                w = pl.ds(low, size)
-                pre_out[w, :] = (part[w, :] + pre_in[w, :].astype(F32)).astype(BF16)
-                pre_copy(c).start()
-
-        @pl.when(sq == S - 1 - k)
-        def _():
-            for c, (low, size) in enumerate(cuts):
-                if k > 0:
-                    suf_copy(c).wait_recv()
-                w = pl.ds(low, size)
-                suf_out[w, :] = (part[w, :] + suf_in[w, :].astype(F32)).astype(BF16)
-                suf_copy(c).start()
-
-    for half in range(4):
-        loop(2 * half, 2 * half + 2, backward)
-        if half == 0:
-            head_part()
-        if half < S - 1:
-            stage(half)
-    for k in range(4, S - 1):
-        stage(k)
+    def pre_on(c):
+        w = pl.ds(*cuts[c])
+        pre_out[w, :] = (part[w, :] + pre_in[w, :].astype(F32)).astype(BF16)
+        pre_copy(c).start()
+
+    def suf_on(c):
+        w = pl.ds(*cuts[c])
+        suf_out[w, :] = (part[w, :] + suf_in[w, :].astype(F32)).astype(BF16)
+        suf_copy(c).start()
+
+    def ends():
+        @pl.when(sq == 0)
+        def _():
+            for c in range(len(cuts)):
+                pre_on(c)
+
+        @pl.when(sq == S - 1)
+        def _():
+            for c in range(len(cuts)):
+                suf_on(c)
+
+    def middle(low, high):
+        @pl.when(jnp.logical_and(has_left, has_right))
+        def _():
+            for c in range(low, high):
+                pre_copy(c).wait_recv()
+                pre_on(c)
+                suf_copy(c).wait_recv()
+                suf_on(c)
+
+    loop(0, 2, backward)
+    head_part()
+    ends()
+    loop(2, 4, backward)
+    middle(0, 2)
+    loop(4, 6, backward)
+    middle(2, 5)
+    loop(6, KV_HEADS, backward)
+    middle(5, len(cuts))
 
     @functools.partial(loop, 0, KV_HEADS)
     def _(j):
@@ -369,8 +400,8 @@
             dv_copy(g).wait_recv()
 
         w = lanes(g, HD)
-        dk_ref[:, w] = (dka[:, w] + dkr[:, w].astype(F32)).astype(BF16)
-        dv_ref[:, w] = (dva[:, w] + dvr[:, w].astype(F32)).astype(BF16)
+        dk_ref[:, w] = (dka[:, w] + dkr[g].astype(F32)).astype(BF16)
+        dv_ref[:, w] = (dva[:, w] + dvr[g].astype(F32)).astype(BF16)
 
     @pl.when(sq == S - 1)
     def _():
@@ -384,7 +415,7 @@
 
     total = part[...] + pre_in[...].astype(F32) + suf_in[...].astype(F32)
     gh_ref[...] = total[:ACTS].T
-    gv_ref[...] = total[ACTS : ACTS + 8]
+    gv_ref[...] = total[ACTS : ACTS + 1]
 
     @pl.when(has_right)
     def _():
@@ -428,6 +459,7 @@
     rows = ACTS + 16
     dma = lambda n: pltpu.SemaphoreType.DMA((n,))
     vm = pltpu.VMEM
+    halo = vm((KV_HEADS, BLOCK, HD), BF16)
     vmem = pl.BlockSpec(memory_space=pltpu.VMEM)
     values_row = jnp.broadcast_to(value_weight[None], (16, FL))
     outs = pl.pallas_call(
@@ -437,12 +469,13 @@
             jax.ShapeDtypeStruct((BLOCK, kw), BF16),
             jax.ShapeDtypeStruct((BLOCK, kw), BF16),
             jax.ShapeDtypeStruct((FL, ACTS), F32),
-            jax.ShapeDtypeStruct((8, FL), F32),
+            jax.ShapeDtypeStruct((1, FL), F32),
         ),
-        in_specs=[vmem] * 7 + [pl.BlockSpec(memory_space=pltpu.SMEM)],
+        in_specs=[pl.BlockSpec(memory_space=pl.ANY)] * 4 + [vmem] * 3 + [pl.BlockSpec(memory_space=pltpu.SMEM)],
         out_specs=(vmem,) * 5,
         scratch_shapes=[
-            vm((BLOCK, kw), BF16), vm((BLOCK, kw), BF16),
+            vm((BLOCK, qw), BF16), vm((BLOCK, kw), BF16), vm((BLOCK, kw), BF16), dma(4),
+            halo, halo,
             vm((qw, ACTS), BF16), vm((D * 16, FL), BF16),
             vm((2 * BLOCK, BLOCK), F32), vm((KV_HEADS, 2 * BLOCK, GW), BF16),
             vm((BLOCK, qw), BF16), vm((D * BLOCK, FL), BF16),
@@ -450,8 +483,7 @@
             vm((8, BLOCK), F32), vm((8, BLOCK), F32),
             vm((BLOCK, ACTS), BF16), vm((BLOCK, BLOCK), F32), vm((D * 8, BLOCK), F32),
             vm((rows, D * BLOCK), BF16),
-            vm((BLOCK, kw), BF16), vm((BLOCK, kw), BF16),
-            vm((BLOCK, kw), BF16), vm((BLOCK, kw), BF16),
+            halo, halo, halo, halo,
             vm((BLOCK, kw), F32), vm((BLOCK, kw), F32),
             vm((rows, FL), F32),
             vm((rows, FL), BF16), vm((rows, FL), BF16), vm((rows, FL), BF16), vm((rows, FL), BF16),
@@ -459,14 +491,14 @@
             dma(D), dma(D), dma(D), dma(D), dma(D), dma(D), dma(D), dma(D), dma(D),
             dma(1), dma(1),
             dma(KV_HEADS), dma(KV_HEADS), dma(KV_HEADS), dma(KV_HEADS),
-            dma(2), dma(2), dma(2), dma(2),
+            dma(8), dma(8), dma(8), dma(8),
         ],
         compiler_params=pltpu.CompilerParams(
-            collective_id=0, has_side_effects=True, vmem_limit_bytes=48 * 2**20
+            collective_id=0, has_side_effects=True, vmem_limit_bytes=60 * 2**20
         ),
     )(queries[0], keys[0], values[0], head_weight, values_row, action_ids, rewards, episode_ids)
     dq, dk, dv, gh, gv = outs
-    return (dq[None], dk[None], dv[None], gh, gv[0])
+    return (dq[None], dk[None], dv[None], gh, gv.reshape(FL))
 
 
 def solution(mesh):

time: 70.3 us -> 100 us (1.42)
  Pallas kernels: 60.2 us -> 93 us
  local copies, waits for them, and re-layouts: 9.17 us -> 6.42 us
    pallas_call x1, Pallas kernels: 60.2 us -> 93 us  [per_device(): pl.pallas_call(functools.partial(kernel, D, S, FL), out_shape=(jax.ShapeD...]
    unnamed x20 -> x15, local copies, waits for them, and re-layouts: 8.59 us -> 5.81 us
where the time goes in v2:
time: 100 us
  Pallas kernels  93 us (93%)
  local copies, waits for them, and re-layouts  6.42 us (6%)
    pallas_call x1, Pallas kernels, per_device(): pl.pallas_call(functools.partial(kernel, D, S, FL), out_shape=(jax.ShapeD...  93 us
    unnamed x15, local copies, waits for them, and re-layouts  5.81 us

profile of v2, /device:TPU:0, one launch (start us, length us, event | category | flops | bytes accessed | tf_op | source)
XLA Modules:
  0.0 100.0 jit_solution(9781101917257049892)
XLA Ops:
  0.6 0.0 copy-start.4
  0.6 0.7 copy-done.4
  1.3 0.6 broadcast_in_dim.15.vw_ref
  1.9 93.0 %shard_map.119 = (bf16[128,4096]{1,0:T(8,128)(2,1)}, bf16[128,1024]{1,0:T(8,128)(2,1)}, bf16[128,1024]{1,0:T(8,128)(2,1)}, f32[512,256]{1,0:T(8,128)}, f32[1,512]{1,0:T(1,128)}) custom-call(bf16[128,4096]{1,0:T(8,128)(2,1)} %bitcast.7, bf16[128,1024]{1,0:T(8,128)(2,1)} %bitcast.11, bf16[128,1024]{1,0:T(8,128)(2,1)} %bitcast.12, bf16[512,256]{1,0:T(8,128)(2,1)} %hw_ref.1, ...), custom_call_target="tpu_custom_call" | custom-call | tf_op jit(solution)/shard_map/pallas_call | solution.py:465
  94.9 0.0 copy-start.2
  94.9 0.0 copy-start.1
  94.9 2.3 %copy.18 = bf16[1,128,4096]{2,1,0:T(8,128)(2,1)} copy(bf16[1,128,4096]{2,1,0:T(8,128)(2,1)} %bitcast.8) | data formatting | bytes 2097152
  97.3 0.0 copy-done.2
  97.3 0.0 copy-start
  97.3 0.7 copy.19
  98.0 0.0 copy-done.1
  98.0 0.7 copy.20
  98.7 0.0 copy-done
  98.7 0.0 copy-start.3
  98.7 0.8 copy.21
  99.5 0.0 copy-done.3
  99.5 0.6 copy.22
Async XLA Ops:
  0.6 0.7 copy-start.4
  94.9 2.4 %copy-start.2 = (bf16[128,1024]{1,0:T(8,128)(2,1)S(1)}, bf16[128,1024]{1,0:T(8,128)(2,1)}, u32[]{:S(2)}) copy-start(bf16[128,1024]{1,0:T(8,128)(2,1)} %get-tuple-element.11) | copy-start | bytes 786436
  94.9 3.1 %copy-start.1 = (bf16[128,1024]{1,0:T(8,128)(2,1)S(1)}, bf16[128,1024]{1,0:T(8,128)(2,1)}, u32[]{:S(2)}) copy-start(bf16[128,1024]{1,0:T(8,128)(2,1)} %get-tuple-element.12) | copy-start | bytes 786436
  97.3 1.4 %copy-start = (f32[512,256]{1,0:T(8,128)S(1)}, f32[512,256]{1,0:T(8,128)}, u32[]{:S(2)}) copy-start(f32[512,256]{1,0:T(8,128)} %get-tuple-element.23) | copy-start | bytes 1572868
  98.7 0.8 copy-start.3

commit v3 on v2

--- a/solution.py
+++ b/solution.py
@@ -56,7 +56,7 @@
     sib = dp + 1 - 2 * (dp % 2)
     R = GW // FL
     rows = ACTS + 16
-    cuts = tuple((32 * c, 32) for c in range(7)) + ((224, rows - 224),)
+    cuts = ((0, 64), (64, 64), (128, 64), (192, rows - 192))
 
     def copy(src, dst, ss, rs, where):
         return pltpu.make_async_remote_copy(
@@ -371,24 +371,45 @@
             for c in range(len(cuts)):
                 suf_on(c)
 
+    def pre_pass(low, high):
+        for c in range(low, high):
+            pre_copy(c).wait_recv()
+            pre_on(c)
+
+    def suf_pass(low, high):
+        for c in range(low, high):
+            suf_copy(c).wait_recv()
+            suf_on(c)
+
+    near_left = jnp.logical_and(has_left, sq < S // 2)
+    near_right = jnp.logical_and(has_right, sq >= S // 2)
+
     def middle(low, high):
-        @pl.when(jnp.logical_and(has_left, has_right))
-        def _():
-            for c in range(low, high):
-                pre_copy(c).wait_recv()
-                pre_on(c)
-                suf_copy(c).wait_recv()
-                suf_on(c)
+        @pl.when(near_left)
+        def _():
+            pre_pass(low, high)
+
+        @pl.when(near_right)
+        def _():
+            suf_pass(low, high)
+
+    def middle_far():
+        @pl.when(near_left)
+        def _():
+            suf_pass(0, len(cuts))
+
+        @pl.when(near_right)
+        def _():
+            pre_pass(0, len(cuts))
 
     loop(0, 2, backward)
     head_part()
     ends()
-    loop(2, 4, backward)
-    middle(0, 2)
-    loop(4, 6, backward)
-    middle(2, 5)
+    loop(2, 6, backward)
+    middle(0, 1)
     loop(6, KV_HEADS, backward)
-    middle(5, len(cuts))
+    middle(1, len(cuts))
+    middle_far()
 
     @functools.partial(loop, 0, KV_HEADS)
     def _(j):
@@ -491,7 +512,7 @@
             dma(D), dma(D), dma(D), dma(D), dma(D), dma(D), dma(D), dma(D), dma(D),
             dma(1), dma(1),
             dma(KV_HEADS), dma(KV_HEADS), dma(KV_HEADS), dma(KV_HEADS),
-            dma(8), dma(8), dma(8), dma(8),
+            dma(4), dma(4), dma(4), dma(4),
         ],
         compiler_params=pltpu.CompilerParams(
             collective_id=0, has_side_effects=True, vmem_limit_bytes=60 * 2**20

time: 100 us -> 63.9 us (0.64)
  Pallas kernels: 93 us -> 56.6 us
    pallas_call x1, Pallas kernels: 93 us -> 56.6 us  [per_device(): pl.pallas_call(functools.partial(kernel, D, S, FL), out_shape=(jax.ShapeD...]
where the time goes in v3:
time: 63.9 us; the launch traced here: 63.7 us
  Pallas kernels  56.6 us (89%)
  local copies, waits for them, and re-layouts  6.42 us (10%)
  between operations  0.67 us (1%)
    pallas_call x1, Pallas kernels, per_device(): pl.pallas_call(functools.partial(kernel, D, S, FL), out_shape=(jax.ShapeD...  56.6 us
    unnamed x15, local copies, waits for them, and re-layouts  5.81 us

profile of v3, /device:TPU:0, one launch (start us, length us, event | category | flops | bytes accessed | tf_op | source)
XLA Modules:
  0.0 63.7 jit_solution(7318854531348919157)
XLA Ops:
  0.6 0.0 copy-start.4
  0.6 0.7 %copy-done.4 = bf16[512]{0:T(512)(128)(2,1)S(1)} copy-done((bf16[512]{0:T(512)(128)(2,1)S(1)}, bf16[512]{0:T(512)(128)(2,1)}, u32[]{:S(2)}) %copy-start.4) | copy-done | bytes 1048
  1.3 0.6 broadcast_in_dim.15.vw_ref
  1.9 56.6 %shard_map.119 = (bf16[128,4096]{1,0:T(8,128)(2,1)}, bf16[128,1024]{1,0:T(8,128)(2,1)}, bf16[128,1024]{1,0:T(8,128)(2,1)}, f32[512,256]{1,0:T(8,128)}, f32[1,512]{1,0:T(1,128)}) custom-call(bf16[128,4096]{1,0:T(8,128)(2,1)} %bitcast.7, bf16[128,1024]{1,0:T(8,128)(2,1)} %bitcast.11, bf16[128,1024]{1,0:T(8,128)(2,1)} %bitcast.12, bf16[512,256]{1,0:T(8,128)(2,1)} %hw_ref.1, ...), custom_call_target="tpu_custom_call" | custom-call | tf_op jit(solution)/shard_map/pallas_call | solution.py:486
  58.5 0.0 copy-start.2
  58.5 0.0 copy-start.1
  58.5 2.3 %copy.18 = bf16[1,128,4096]{2,1,0:T(8,128)(2,1)} copy(bf16[1,128,4096]{2,1,0:T(8,128)(2,1)} %bitcast.8) | data formatting | bytes 2097152
  60.9 0.0 copy-done.2
  60.9 0.0 copy-start
  60.9 0.7 %copy.19 = bf16[1,128,1024]{2,1,0:T(8,128)(2,1)} copy(bf16[1,128,1024]{2,1,0:T(8,128)(2,1)S(1)} %bitcast.10) | data formatting | bytes 524288
  61.6 0.0 copy-done.1
  61.6 0.7 %copy.20 = bf16[1,128,1024]{2,1,0:T(8,128)(2,1)} copy(bf16[1,128,1024]{2,1,0:T(8,128)(2,1)S(1)} %bitcast.9) | data formatting | bytes 524288
  62.3 0.0 copy-done
  62.3 0.0 copy-start.3
  62.3 0.8 %copy.21 = f32[512,256]{1,0:T(8,128)} copy(f32[512,256]{1,0:T(8,128)S(1)} %copy-done) | data formatting | bytes 1048576
  63.1 0.0 copy-done.3
  63.1 0.6 copy.22
Async XLA Ops:
  0.6 0.7 %copy-start.4 = (bf16[512]{0:T(512)(128)(2,1)S(1)}, bf16[512]{0:T(512)(128)(2,1)}, u32[]{:S(2)}) copy-start(bf16[512]{0:T(512)(128)(2,1)} %param.12) | copy-start | bytes 3076
  58.5 2.4 %copy-start.2 = (bf16[128,1024]{1,0:T(8,128)(2,1)S(1)}, bf16[128,1024]{1,0:T(8,128)(2,1)}, u32[]{:S(2)}) copy-start(bf16[128,1024]{1,0:T(8,128)(2,1)} %get-tuple-element.11) | copy-start | bytes 786436
  58.5 3.1 %copy-start.1 = (bf16[128,1024]{1,0:T(8,128)(2,1)S(1)}, bf16[128,1024]{1,0:T(8,128)(2,1)}, u32[]{:S(2)}) copy-start(bf16[128,1024]{1,0:T(8,128)(2,1)} %get-tuple-element.12) | copy-start | bytes 786436
  60.9 1.4 %copy-start = (f32[512,256]{1,0:T(8,128)S(1)}, f32[512,256]{1,0:T(8,128)}, u32[]{:S(2)}) copy-start(f32[512,256]{1,0:T(8,128)} %get-tuple-element.23) | copy-start | bytes 1572868
  62.3 0.8 %copy-start.3 = (f32[1,512]{1,0:T(1,128)S(1)}, f32[1,512]{1,0:T(1,128)}, u32[]{:S(2)}) copy-start(f32[1,512]{1,0:T(1,128)} %get-tuple-element.14) | copy-start | bytes 6148

commit v4 on v3

--- a/solution.py
+++ b/solution.py
@@ -402,13 +402,11 @@
         def _():
             pre_pass(0, len(cuts))
 
-    loop(0, 2, backward)
+    loop(0, 6, backward)
     head_part()
     ends()
-    loop(2, 6, backward)
-    middle(0, 1)
     loop(6, KV_HEADS, backward)
-    middle(1, len(cuts))
+    middle(0, len(cuts))
     middle_far()
 
     @functools.partial(loop, 0, KV_HEADS)

time: 63.9 us -> 59.4 us (0.930)
  Pallas kernels: 56.6 us -> 52.1 us
    pallas_call x1, Pallas kernels: 56.6 us -> 52.1 us  [per_device(): pl.pallas_call(functools.partial(kernel, D, S, FL), out_shape=(jax.ShapeD...]
where the time goes in v4:
time: 59.4 us; the launch traced here: 59.2 us
  Pallas kernels  52.1 us (88%)
  local copies, waits for them, and re-layouts  6.42 us (11%)
  between operations  0.67 us (1%)
    pallas_call x1, Pallas kernels, per_device(): pl.pallas_call(functools.partial(kernel, D, S, FL), out_shape=(jax.ShapeD...  52.1 us
    unnamed x15, local copies, waits for them, and re-layouts  5.81 us

profile of v4, /device:TPU:0, one launch (start us, length us, event | category | flops | bytes accessed | tf_op | source)
XLA Modules:
  0.0 59.2 jit_solution(9181082925599026794)
XLA Ops:
  0.6 0.0 copy-start.4
  0.6 0.7 %copy-done.4 = bf16[512]{0:T(512)(128)(2,1)S(1)} copy-done((bf16[512]{0:T(512)(128)(2,1)S(1)}, bf16[512]{0:T(512)(128)(2,1)}, u32[]{:S(2)}) %copy-start.4) | copy-done | bytes 1048
  1.3 0.6 %broadcast_in_dim.15.vw_ref = bf16[16,512]{1,0:T(8,128)(2,1)} broadcast(bf16[512]{0:T(512)(128)(2,1)S(1)} %copy-done.4), dimensions={1} | broadcast | bytes 17408 | tf_op jit(solution)/shard_map/broadcast_in_dim | solution.py:483
  1.9 52.1 %shard_map.119 = (bf16[128,4096]{1,0:T(8,128)(2,1)}, bf16[128,1024]{1,0:T(8,128)(2,1)}, bf16[128,1024]{1,0:T(8,128)(2,1)}, f32[512,256]{1,0:T(8,128)}, f32[1,512]{1,0:T(1,128)}) custom-call(bf16[128,4096]{1,0:T(8,128)(2,1)} %bitcast.7, bf16[128,1024]{1,0:T(8,128)(2,1)} %bitcast.11, bf16[128,1024]{1,0:T(8,128)(2,1)} %bitcast.12, bf16[512,256]{1,0:T(8,128)(2,1)} %hw_ref.1, ...), custom_call_target="tpu_custom_call" | custom-call | tf_op jit(solution)/shard_map/pallas_call | solution.py:484
  54.0 0.0 copy-start.2
  54.0 0.0 copy-start.1
  54.0 2.3 %copy.18 = bf16[1,128,4096]{2,1,0:T(8,128)(2,1)} copy(bf16[1,128,4096]{2,1,0:T(8,128)(2,1)} %bitcast.8) | data formatting | bytes 2097152
  56.4 0.0 copy-done.2
  56.4 0.0 copy-start
  56.4 0.7 %copy.19 = bf16[1,128,1024]{2,1,0:T(8,128)(2,1)} copy(bf16[1,128,1024]{2,1,0:T(8,128)(2,1)S(1)} %bitcast.10) | data formatting | bytes 524288
  57.1 0.0 copy-done.1
  57.1 0.7 %copy.20 = bf16[1,128,1024]{2,1,0:T(8,128)(2,1)} copy(bf16[1,128,1024]{2,1,0:T(8,128)(2,1)S(1)} %bitcast.9) | data formatting | bytes 524288
  57.8 0.0 copy-done
  57.8 0.0 copy-start.3
  57.8 0.8 %copy.21 = f32[512,256]{1,0:T(8,128)} copy(f32[512,256]{1,0:T(8,128)S(1)} %copy-done) | data formatting | bytes 1048576
  58.6 0.0 copy-done.3
  58.6 0.6 copy.22
Async XLA Ops:
  0.6 0.7 %copy-start.4 = (bf16[512]{0:T(512)(128)(2,1)S(1)}, bf16[512]{0:T(512)(128)(2,1)}, u32[]{:S(2)}) copy-start(bf16[512]{0:T(512)(128)(2,1)} %param.12) | copy-start | bytes 3076
  54.0 2.4 %copy-start.2 = (bf16[128,1024]{1,0:T(8,128)(2,1)S(1)}, bf16[128,1024]{1,0:T(8,128)(2,1)}, u32[]{:S(2)}) copy-start(bf16[128,1024]{1,0:T(8,128)(2,1)} %get-tuple-element.11) | copy-start | bytes 786436
  54.0 3.1 %copy-start.1 = (bf16[128,1024]{1,0:T(8,128)(2,1)S(1)}, bf16[128,1024]{1,0:T(8,128)(2,1)}, u32[]{:S(2)}) copy-start(bf16[128,1024]{1,0:T(8,128)(2,1)} %get-tuple-element.12) | copy-start | bytes 786436
  56.4 1.4 %copy-start = (f32[512,256]{1,0:T(8,128)S(1)}, f32[512,256]{1,0:T(8,128)}, u32[]{:S(2)}) copy-start(f32[512,256]{1,0:T(8,128)} %get-tuple-element.23) | copy-start | bytes 1572868
  57.8 0.8 %copy-start.3 = (f32[1,512]{1,0:T(1,128)S(1)}, f32[1,512]{1,0:T(1,128)}, u32[]{:S(2)}) copy-start(f32[1,512]{1,0:T(1,128)} %get-tuple-element.14) | copy-start | bytes 6148
